TPU v7x, 1024 devices: a whole 4x8x16 slice. The times are simulated.
1024 devices in a mesh: feat: 16 (over z), dp: 64 (over y, x, core).
Axes of the slice: x: 4, y: 8, z: 16, core: 2. Of those that a mesh axis runs over, the one named last changes fastest.
Arguments:
- targets_x: bfloat16 [1024, 131072], P('feat', 'dp'), may hold values from -6 to 6
- frontier: bfloat16 [1024, 393216], P('feat', 'dp'), may hold values from -6 to 6
- neighbours1: int32 [10, 131072], P(None, 'dp'), may hold values from 0 to 6143
- counts1: int32 [131072], P('dp'), may hold values from 1 to 10
- w1_self: bfloat16 [1024, 256], P('feat'), may hold values from -0.125 to 0.125
- w1_neigh: bfloat16 [1024, 256], P('feat'), may hold values from -0.1875 to 0.1875
- history: bfloat16 [524288, 256], P(('dp', 'feat')), may hold values from -6 to 6
- neighbours2: int32 [25, 131072], P(None, ('dp', 'feat')), may hold values from 0 to 511
- counts2: int32 [131072], P(('dp', 'feat')), may hold values from 1 to 25
- w2_self: bfloat16 [256, 256], replicated, may hold values from -0.375 to 0.375
- w2_neigh: bfloat16 [256, 256], replicated, may hold values from -0.375 to 0.375
- out_grad: bfloat16 [131072, 256], P(('dp', 'feat')), may hold values from -6 to 6
Outputs:
- logits: bfloat16 [131072, 256], P(('dp', 'feat'))
- grad_w1_self: float32 [1024, 256], P('feat')
- grad_w1_neigh: float32 [1024, 256], P('feat')
- grad_w2_self: float32 [256, 256], replicated
- grad_w2_neigh: float32 [256, 256], replicated
All inputs are finite; a program needn't handle non-finite values.
Results may differ from a plain program's by a relative error of at most 0.0051.
Values may be sent and summed in bfloat16 or wider, within the bound.
A program may use at most 32 MiB of HBM per device.

v0:
```python
import jax
import jax.numpy as jnp
from jax import lax
from jax.sharding import PartitionSpec as P


def mean_columns(lookup, col_ids, counts):
    picked = lookup[:, col_ids]
    usable = lax.broadcasted_iota(jnp.int32, col_ids.shape, 0) < counts[None, :]
    summed = jnp.sum(
        jnp.where(usable[None, :, :], picked, jnp.zeros((), picked.dtype)),
        axis=1,
        dtype=jnp.float32,
    )
    return (summed / counts[None, :].astype(jnp.float32)).astype(jnp.bfloat16)


def mean_history(lookup, row_ids, counts):
    picked = lookup[row_ids]
    usable = lax.broadcasted_iota(jnp.int32, row_ids.shape, 0) < counts[None, :]
    summed = jnp.sum(
        jnp.where(usable[:, :, None], picked, jnp.zeros((), picked.dtype)),
        axis=0,
        dtype=jnp.float32,
    )
    return (summed / counts[:, None].astype(jnp.float32)).astype(jnp.bfloat16)


def silu_slope(pre_act):
    sigmoid_val = jax.nn.sigmoid(pre_act)
    return sigmoid_val * (1.0 + pre_act * (1.0 - sigmoid_val))


def contract_rows(left, right):
    return lax.dot_general(
        left, right, (((0,), (0,)), ((), ())), preferred_element_type=jnp.float32
    )


def local(
    targets_x,
    frontier,
    neighbours1,
    counts1,
    w1_self,
    w1_neigh,
    history,
    neighbours2,
    counts2,
    w2_self,
    w2_neigh,
    out_grad,
):
    agg_one = mean_columns(frontier, neighbours1, counts1)
    agg_two = mean_history(history, neighbours2, counts2)
    self_cols = targets_x
    neigh_cols = agg_one
    pre_act = lax.psum_scatter(
        contract_rows(self_cols, w1_self) + contract_rows(neigh_cols, w1_neigh),
        "feat",
        scatter_dimension=0,
        tiled=True,
    )
    hidden = jax.nn.silu(pre_act).astype(jnp.bfloat16)
    logits = (
        jnp.dot(hidden, w2_self, preferred_element_type=jnp.float32)
        + jnp.dot(agg_two, w2_neigh, preferred_element_type=jnp.float32)
    ).astype(jnp.bfloat16)
    later_self, later_neigh = lax.psum(
        (contract_rows(hidden, out_grad), contract_rows(agg_two, out_grad)), ("feat", "dp")
    )
    back = lax.dot_general(
        out_grad, w2_self, (((1,), (1,)), ((), ())), preferred_element_type=jnp.float32
    )
    pre_grad = (back * silu_slope(pre_act)).astype(jnp.bfloat16)
    grad_piece = lax.all_gather(pre_grad, "feat", axis=0, tiled=True)
    self_cols = targets_x
    neigh_cols = agg_one
    slice_self = jnp.dot(self_cols, grad_piece, preferred_element_type=jnp.float32)
    slice_neigh = jnp.dot(neigh_cols, grad_piece, preferred_element_type=jnp.float32)
    grad_self, grad_neigh = lax.psum((slice_self, slice_neigh), "dp")
    return (logits, grad_self, grad_neigh, later_self, later_neigh)


def solution(mesh):
    return jax.shard_map(
        local,
        mesh=mesh,
        in_specs=(
            P("feat", "dp"),
            P("feat", "dp"),
            P(None, "dp"),
            P("dp"),
            P("feat", None),
            P("feat", None),
            P(("dp", "feat"), None),
            P(None, ("dp", "feat")),
            P(("dp", "feat")),
            P(),
            P(),
            P(("dp", "feat"), None),
        ),
        out_specs=(P(("dp", "feat"), None), P("feat", None), P("feat", None), P(), P()),
        check_vma=False,
    )
```

profile of v0, /device:TPU:1, one launch (start us, length us, event | category | flops | bytes accessed | tf_op | source)
XLA Modules:
  0.0 956.9 jit_solution(9657317639285990586)
XLA Ops:
  7.2 0.0 copy-start
  7.2 0.0 copy-start.2
  7.2 0.0 reduce-scatter.2.cloned.1.call-start
  7.2 0.8 iota_compare_fusion
  8.0 0.7 convert_element_type.30
  8.7 1.8 copy.17
  10.5 0.0 copy-done.2
  10.6 72.2 %gather_fusion = bf16[20480,64]{1,0:T(8,128)(2,1)} fusion(bf16[64,6144]{0,1:T(8,128)(2,1)S(1)} %copy.17, s32[20480]{0:T(1024)S(1)} %broadcast_clamp_fusion), kind=kCustom, calls=%fused_computation | custom fusion | bytes 5324800 | tf_op jit(solution)/shard_map/gather | solution.py:8
  82.7 0.0 copy-start.4
  82.7 7.6 convert_reduce_fusion
  90.3 0.0 copy-start.1
  90.3 0.0 copy-start.3
  90.3 0.3 divide_convert_fusion
  90.7 0.0 copy-done.4
  90.7 0.4 fusion.6
  91.1 0.2 copy-done.1
  91.3 0.0 copy-done.3
  91.3 1.8 convolution_add_fusion
  93.1 0.0 copy-start.7
  93.1 0.0 copy-start.10
  93.1 0.0 copy-start.6
  93.1 0.0 copy-start.5
  93.1 0.0 reduce-scatter.2.cloned.1.call-update
  93.1 0.0 all-gather.2.cloned.1.call-start
  93.2 75.6 %reduce-scatter.2.cloned.1.call-done = f32[128,256]{1,0:T(8,128)} async-done(((f32[2048,256]{1,0:T(8,128)}), f32[128,256]{1,0:T(8,128)}) %reduce-scatter.2.cloned.1.call-update) | async-done | bytes 131088 | tf_op jit(solution)/shard_map/reduce_scatter | solution.py:58
  168.8 0.0 copy-done.7
  168.8 0.0 copy-done.10
  168.8 1.7 fusion.1
  170.5 0.0 all-gather.2.cloned.1.call-update
  170.5 0.0 all-reduce.5.cloned.1.call-start
  170.6 0.0 copy-done.6
  170.6 0.0 copy-done.5
  170.6 0.0 copy-done
  170.7 9.9 %gather_fusion.1 = bf16[3200,256]{1,0:T(8,128)(2,1)S(1)} fusion(bf16[512,256]{1,0:T(8,128)(2,1)S(1)} %copy-done, s32[4096]{0:T(1024)S(1)} %pad_clamp_fusion), kind=kCustom, calls=%fused_computation.1 | custom fusion | bytes 3289600 | tf_op jit(solution)/shard_map/gather | solution.py:19
  180.6 0.0 copy-start.9
  180.6 0.6 convert_reduce_fusion.1
  181.3 1.0 fusion.5
  182.2 0.0 copy-done.9
  182.2 0.9 fusion.3
  183.2 0.0 copy-start.8
  183.2 0.0 all-reduce.5.cloned.1.call-update
  183.2 0.0 all-reduce.7.cloned.1.call-start
  183.3 0.2 fusion.4
  183.4 61.4 %all-gather.2.cloned.1.call-done = bf16[2048,256]{1,0:T(8,128)(2,1)} async-done(((bf16[128,256]{1,0:T(8,128)(2,1)}), bf16[2048,256]{1,0:T(8,128)(2,1)}) %all-gather.2.cloned.1.call-update) | async-done | bytes 1048592 | tf_op jit(solution)/shard_map/all_gather | solution.py:76
  244.8 2.2 fusion.7
  247.0 2.2 convolution_bitcast_fusion
  249.1 0.0 all-reduce.7.cloned.1.call-update
  249.1 0.0 copy-done.8
  249.2 0.9 fusion
  250.0 486.0 %all-reduce.5.cloned.1.call-done = (f32[256,256]{1,0:T(8,128)}, f32[256,256]{1,0:T(8,128)}) async-done(((f32[256,256]{1,0:T(8,128)}, f32[256,256]{1,0:T(8,128)}), (f32[256,256]{1,0:T(8,128)}, f32[256,256]{1,0:T(8,128)})) %all-reduce.5.cloned.1.call-update) | async-done | bytes 524304 | tf_op jit(solution)/shard_map/psum | solution.py:69
  736.0 208.1 %all-reduce.7.cloned.1.call-done = (f32[64,256]{1,0:T(8,128)}, f32[64,256]{1,0:T(8,128)}) async-done(((f32[64,256]{1,0:T(8,128)}, f32[64,256]{1,0:T(8,128)}), (f32[64,256]{1,0:T(8,128)}, f32[64,256]{1,0:T(8,128)})) %all-reduce.7.cloned.1.call-update) | async-done | bytes 131088 | tf_op jit(solution)/shard_map/psum | solution.py:81
  944.0 1.5 copy.22
  945.5 1.5 copy.23
  947.0 1.7 copy.24
  948.7 1.7 copy.25
  (7 shorter events, 0.1 us)
Async XLA Ops:
  7.2 163.5 %copy-start = (bf16[512,256]{1,0:T(8,128)(2,1)S(1)}, bf16[512,256]{1,0:T(8,128)(2,1)}, u32[]{:S(2)}) copy-start(bf16[512,256]{1,0:T(8,128)(2,1)} %param.18) | copy-start | bytes 786436
  7.2 3.3 copy-start.2
  7.2 161.6 %reduce-scatter.2.cloned.1.call-start = ((), (), s32[]{:S(2)}) async-start(), calls=%async_computation.1 | async-start | bytes 2228224 | tf_op jit(solution)/shard_map/reduce_scatter | solution.py:58
  82.7 8.0 copy-start.4
  90.3 1.0 copy-start.1
  90.3 0.9 copy-start.3
  93.1 75.7 %copy-start.7 = (bf16[256,256]{1,0:T(8,128)(2,1)S(1)}, bf16[256,256]{1,0:T(8,128)(2,1)}, u32[]{:S(2)}) copy-start(bf16[256,256]{1,0:T(8,128)(2,1)} %param.21) | copy-start | bytes 393220
  93.1 75.7 %copy-start.10 = (bf16[128,256]{1,0:T(8,128)(2,1)S(1)}, bf16[128,256]{1,0:T(8,128)(2,1)}, u32[]{:S(2)}) copy-start(bf16[128,256]{1,0:T(8,128)(2,1)} %param.23) | copy-start | bytes 196612
  93.1 77.5 %copy-start.6 = (s32[128]{0:T(128)S(1)}, s32[128]{0:T(128)}, u32[]{:S(2)}) copy-start(s32[128]{0:T(128)} %param.20) | copy-start | bytes 1540
  93.1 77.5 %copy-start.5 = (s32[25,128]{1,0:T(8,128)S(1)}, s32[25,128]{1,0:T(8,128)}, u32[]{:S(2)}) copy-start(s32[25,128]{1,0:T(8,128)} %param.19) | copy-start | bytes 38404
  93.1 151.7 %all-gather.2.cloned.1.call-start = ((), (), s32[]{:S(2)}) async-start(), calls=%async_computation.2 | async-start | bytes 1114112 | tf_op jit(solution)/shard_map/all_gather | solution.py:76
  170.5 565.4 %all-reduce.5.cloned.1.call-start = ((), (), s32[]{:S(2)}) async-start(), calls=%async_computation.3 | async-start | bytes 1048576 | tf_op jit(solution)/shard_map/psum | solution.py:69
  180.6 1.7 copy-start.9
  183.2 66.0 %copy-start.8 = (bf16[256,256]{1,0:T(8,128)(2,1)S(1)}, bf16[256,256]{1,0:T(8,128)(2,1)}, u32[]{:S(2)}) copy-start(bf16[256,256]{1,0:T(8,128)(2,1)} %param.22) | copy-start | bytes 393220
  183.2 760.8 %all-reduce.7.cloned.1.call-start = ((), (), s32[]{:S(2)}) async-start(), calls=%async_computation.4 | async-start | bytes 262144 | tf_op jit(solution)/shard_map/psum | solution.py:81
Sparse Core Ops, SparseCore 0:
  93.2 75.4 reduce-scatter.1
  172.0 72.7 all-gather.1
  251.0 484.9 all-reduce.4
  739.9 204.0 all-reduce.6
where the time goes:
time: 957 us
  waiting for transfers between devices  831 us (87%)
  local copies, waits for them, and re-layouts  90.4 us (9%)
  between operations  14 us (1%)
  matrix products  11.2 us (1%)
  other arithmetic  10.1 us (1%)
    psum x1, waiting for transfers between devices, local(): lax.psum((contract_rows(hidden, out_grad), contract_rows(agg_two, out_gra...  486 us
    psum x1, waiting for transfers between devices, local(): grad_self, grad_neigh = lax.psum((slice_self, slice_neigh), 'dp')  208 us
    reduce_scatter x1, waiting for transfers between devices, local(): lax.psum_scatter(contract_rows(self_cols, w1_self) + contract_rows(neigh_...  75.6 us
    gather x1, local copies, waits for them, and re-layouts, mean_columns(): picked = lookup[:, col_ids]  72.2 us
    all_gather x1, waiting for transfers between devices, local(): grad_piece = lax.all_gather(pre_grad, 'feat', axis=0, tiled=True)  61.4 us
  transfers between devices with their start and end apart: 4, of which 4 were waited for; matrix products, arithmetic and copies ran while one was open for 2% of the time, Pallas kernels for 0%

commit v1 on v0

v1 whole, which is shorter than its diff:
```python
import functools

import jax
import jax.numpy as jnp
from jax import lax
from jax.experimental import pallas as pl
from jax.experimental.pallas import tpu as pltpu
from jax.sharding import PartitionSpec as P

MESH = pl.DeviceIdType.MESH
F32, BF16 = jnp.float32, jnp.bfloat16


def dot(left, right):
    return jnp.dot(left, right, preferred_element_type=F32)


def dot_rows(left, right):
    return lax.dot_general(left, right, (((0,), (0,)), ((), ())), preferred_element_type=F32)


def gather_kernel(
    slots, unroll, idx_ref, cnt_ref, f_ref, tx_ref, hist_ref, n2_ref, c2_ref,
    x_ref, xt_ref, a2_ref, tab, rows,
):
    width, nodes = f_ref.shape
    targets = tx_ref.shape[1]
    tab[nodes : nodes + 8, :] = jnp.zeros((8, 128), F32)

    def turn(i, carry):
        at = pl.multiple_of(i * 128, 128)
        tab[pl.ds(at, 128), 0:width] = f_ref[:, pl.ds(at, 128)].astype(F32).T
        return carry

    lax.fori_loop(0, nodes // 128, turn, 0, unroll=4)

    def pick(i, carry):
        for u in range(unroll):
            t = i * unroll + u
            terms = [tab[pl.ds(idx_ref[k * targets + t], 1), :] for k in range(slots)]
            while len(terms) > 1:
                odd = terms[-1:] if len(terms) % 2 else []
                terms = [a + b for a, b in zip(terms[::2], terms[1::2])] + odd
            rows[pl.ds(t, 1), :] = terms[0]
        return carry

    lax.fori_loop(0, targets // unroll, pick, 0)

    def finish(c, carry):
        at = pl.multiple_of(c * 128, 128)
        mean = rows[pl.ds(at, 128), :].T[0:width, :] / cnt_ref[:, pl.ds(at, 128)].astype(F32)
        both = jnp.concatenate([tx_ref[:, pl.ds(at, 128)].astype(F32), mean], axis=0)
        x_ref[c] = both.astype(BF16)
        xt_ref[c] = both.T.astype(BF16)
        return carry

    lax.fori_loop(0, targets // 128, finish, 0)

    c2 = c2_ref[...]
    node = lax.broadcasted_iota(jnp.int32, (hist_ref.shape[0], c2.shape[1]), 0)
    times = jnp.zeros(node.shape, F32)
    for k in range(n2_ref.shape[0]):
        live = jnp.where(k < c2, n2_ref[k : k + 1, :], -1)
        times = times + jnp.where(node == live, 1.0, 0.0)
    total = dot_rows(hist_ref[...], times.astype(BF16))
    a2_ref[...] = (total / c2.astype(F32)).T.astype(BF16)


def gather_means(tx, frontier, n1, c1, history, n2, c2):
    slots, targets = n1.shape
    live = lax.broadcasted_iota(jnp.int32, n1.shape, 0) < c1[None, :]
    idx = jnp.where(live, n1, frontier.shape[1]).reshape(-1)
    chunks = targets // 128
    deep = 2 * tx.shape[0]
    vmem = pl.BlockSpec(memory_space=pltpu.VMEM)
    return pl.pallas_call(
        functools.partial(gather_kernel, slots, 32),
        out_shape=(
            jax.ShapeDtypeStruct((chunks, deep, 128), BF16),
            jax.ShapeDtypeStruct((chunks, 128, deep), BF16),
            jax.ShapeDtypeStruct((c2.shape[0], history.shape[1]), BF16),
        ),
        in_specs=[pl.BlockSpec(memory_space=pltpu.SMEM)] + [vmem] * 6,
        out_specs=(vmem,) * 3,
        scratch_shapes=[
            pltpu.VMEM((frontier.shape[1] + 8, 128), F32),
            pltpu.VMEM((targets, 128), F32),
        ],
        compiler_params=pltpu.CompilerParams(vmem_limit_bytes=24 << 20),
    )(idx, c1.reshape(1, -1), frontier, tx, history, n2, c2.reshape(1, -1))


class Spread:
    def __init__(self, size, mine, device):
        self.size, self.mine, self.device = size, mine, device

    def peer(self, offset):
        return lax.rem(self.mine + offset, self.size)

    def copies(self, sems, source, target):
        send, recv = sems
        return [
            pltpu.make_async_remote_copy(
                src_ref=source(self.peer(o)),
                dst_ref=target(o),
                send_sem=send.at[o - 1],
                recv_sem=recv.at[o - 1],
                device_id=self.device(self.peer(o)),
                device_id_type=MESH,
            )
            for o in range(1, self.size)
        ]

    def greet(self, barrier):
        for o in range(1, self.size):
            pl.semaphore_signal(
                barrier, inc=1, device_id=self.device(self.peer(o)), device_id_type=MESH
            )


class Total:
    def __init__(self, groups, refs, own, out):
        self.xc, self.y, self.za, self.zb = groups
        (self.rxc, self.vy, self.ry, self.va, self.vb, self.fy, self.fo) = refs[:7]
        sems = refs[7:]
        self.sems = [(sems[2 * i], sems[2 * i + 1]) for i in range(6)]
        self.own, self.out = own, out
        self.live = None
        self.all = []

    def launch(self, copies):
        for copy in copies:
            copy.start()
        self.live = copies
        self.all += copies

    def arrive(self):
        for copy in self.live:
            copy.wait_recv()

    def stage(self, number):
        if number == 0:
            self.launch(self.xc.copies(self.sems[0], lambda p: self.own.at[p], lambda o: self.rxc.at[o - 1]))
            return
        self.arrive()
        if number == 1:
            total = self.own[self.xc.mine]
            for o in range(self.xc.size - 1):
                total = total + self.rxc[o]
            part = self.vy.shape[1]
            for j in range(self.y.size):
                self.vy[j] = total[j * part : (j + 1) * part]
            self.launch(self.y.copies(self.sems[1], lambda p: self.vy.at[p], lambda o: self.ry.at[o - 1]))
        elif number == 2:
            total = self.vy[self.y.mine]
            for o in range(self.y.size - 1):
                total = total + self.ry[o]
            me = self.za.mine
            self.va[me] = total
            self.launch(self.za.copies(self.sems[2], lambda p: self.va.at[me], lambda o: self.va.at[me]))
        elif number == 3:
            total = self.va[0]
            for j in range(1, self.za.size):
                total = total + self.va[j]
            me = self.zb.mine
            self.vb[me] = total
            self.launch(self.zb.copies(self.sems[3], lambda p: self.vb.at[me], lambda o: self.vb.at[me]))
        elif number == 4:
            total = self.vb[0]
            for j in range(1, self.zb.size):
                total = total + self.vb[j]
            me = self.y.mine
            self.fy[me] = total
            self.launch(self.y.copies(self.sems[4], lambda p: self.fy.at[me], lambda o: self.fy.at[me]))
        elif number == 5:
            me = self.xc.mine
            self.launch(self.xc.copies(self.sems[5], lambda p: self.fy, lambda o: self.fo.at[me]))
            self.fo[me] = self.fy[...]
        else:
            part = self.fo.shape[2]
            for q in range(self.xc.size):
                for j in range(self.y.size):
                    at = (q * self.y.size + j) * part
                    self.out[at : at + part, :] = self.fo[q, j]
            for copy in self.all:
                copy.wait_send()


def exchange_kernel(shape, names, *refs):
    nz, ny, nq, zblock = shape
    r = dict(zip(names, refs))
    z = lax.axis_index("feat")
    dp = lax.axis_index("dp")
    q, y = lax.rem(dp, nq), lax.div(dp, nq)
    za, zb = lax.rem(z, zblock), lax.div(z, zblock)
    wrap = lambda v: lax.rem(v + 2 * nz, nz)

    group_q = Spread(nq, q, lambda p: (z, y * nq + p))
    group_y = Spread(ny, y, lambda p: (z, p * nq + q))
    group_a = Spread(zblock, za, lambda p: (zb * zblock + p, dp))
    group_b = Spread(nz // zblock, zb, lambda p: (p * zblock + za, dp))
    groups = (group_q, group_y, group_a, group_b)
    right, left = (wrap(z + 1), dp), (wrap(z - 1), dp)

    barrier = pltpu.get_barrier_semaphore()
    for neighbour in (left, right):
        pl.semaphore_signal(barrier, inc=1, device_id=neighbour, device_id_type=MESH)
    for group in groups:
        group.greet(barrier)

    x, xt, w, og, agg2 = r["x"], r["xt"], r["w"], r["og"], r["agg2"]
    part = r["part"]
    half = xt.shape[1] // 2
    steps_r, steps_l = nz // 2, nz // 2 - 1

    def make_part(j):
        c = wrap(z - steps_l + j)
        part[c] = dot(xt[c], w[...])

    make_part(0)
    make_part(nz - 1)
    out_r, out_l, in_r, in_l = r["out_r"], r["out_l"], r["in_r"], r["in_l"]

    def ring_copy(source, target, sems, s, h, device):
        return pltpu.make_async_remote_copy(
            src_ref=source,
            dst_ref=target.at[s, h],
            send_sem=sems[0].at[s, h],
            recv_sem=sems[1].at[s, h],
            device_id=device,
            device_id_type=MESH,
        )

    sems_r, sems_l = (r["rs_rs"], r["rs_rr"]), (r["rs_ls"], r["rs_lr"])
    rs_r = [[ring_copy(out_r.at[s, h], in_r, sems_r, s, h, right) for h in range(2)] for s in range(steps_r)]
    rs_l = [[ring_copy(out_l.at[s, h], in_l, sems_l, s, h, left) for h in range(2)] for s in range(steps_l)]

    def put(copies, out, arrived, s, h, c):
        value = part[c, h * half : (h + 1) * half, :]
        if s > 0:
            copies[s - 1][h].wait_recv()
            value = value + arrived[s - 1, h].astype(F32)
        out[s, h] = value.astype(BF16)
        copies[s][h].start()

    own_n, own_s = r["own_n"], r["own_s"]
    nparts = own_n.shape[0]
    rows_q = own_n.shape[1]

    def store_own(own, value):
        for j in range(nparts):
            own[j] = value[j * rows_q : (j + 1) * rows_q]

    neigh = Total(groups, [r["n_" + n] for n in TOTAL_NAMES], own_n, r["gn"])
    itself = Total(groups, [r["s_" + n] for n in TOTAL_NAMES], own_s, r["gs"])

    pl.semaphore_wait(barrier, 2 + sum(group.size - 1 for group in groups))

    for h in range(2):
        put(rs_r, out_r, in_r, 0, h, wrap(z + steps_r))
        put(rs_l, out_l, in_l, 0, h, wrap(z - steps_l))

    def rest(j, carry):
        make_part(j)
        return carry

    lax.fori_loop(1, nz - 1, rest, 0)
    store_own(own_n, dot_rows(agg2[...], og[...]))
    neigh.stage(0)
    r["back"][...] = lax.dot_general(
        og[...], r["w2s"][...], (((1,), (1,)), ((), ())), preferred_element_type=F32
    )

    plan_n, plan_s = NEIGH_PLAN[nz], SELF_PLAN[nz]
    for s in range(1, steps_r):
        for h in range(2):
            put(rs_r, out_r, in_r, s, h, wrap(z + steps_r - s))
            if s < steps_l:
                put(rs_l, out_l, in_l, s, h, wrap(z - steps_l + s))
        for number in plan_n.get(s, ()):
            neigh.stage(number)

    ag_r, ag_l, pg, hid = r["ag_r"], r["ag_l"], r["pg"], r["hid"]
    sems_gr, sems_gl = (r["ag_rs"], r["ag_rr"]), (r["ag_ls"], r["ag_lr"])
    fw_r = [[ring_copy(pg.at[h] if s == 0 else ag_r.at[s - 1, h], ag_r, sems_gr, s, h, right) for h in range(2)] for s in range(steps_r)]
    fw_l = [[ring_copy(pg.at[h] if s == 0 else ag_l.at[s - 1, h], ag_l, sems_gl, s, h, left) for h in range(2)] for s in range(steps_l)]

    for h in range(2):
        rs_l[steps_l - 1][h].wait_recv()
        rs_r[steps_r - 1][h].wait_recv()
        span = slice(h * half, (h + 1) * half)
        pre = part[z, span, :] + (in_r[steps_r - 1, h].astype(F32) + in_l[steps_l - 1, h].astype(F32))
        sig = 1.0 / (1.0 + jnp.exp(-pre))
        pg[h] = (r["back"][span, :] * (sig * (1.0 + pre * (1.0 - sig)))).astype(BF16)
        fw_r[0][h].start()
        fw_l[0][h].start()
        hid[span, :] = (pre * sig).astype(BF16)

    store_own(own_s, dot_rows(hid[...], og[...]))
    itself.stage(0)
    r["logits"][...] = (dot(hid[...], r["w2s"][...]) + dot(agg2[...], r["w2n"][...])).astype(BF16)
    for number in plan_n.get("mid", ()):
        neigh.stage(number)

    def term(c, block):
        return dot(x[c], jnp.concatenate([block[0], block[1]], axis=0))

    grad = term(z, pg)
    for s in range(steps_r):
        for h in range(2):
            fw_r[s][h].wait_recv()
            if s + 1 < steps_r:
                fw_r[s + 1][h].start()
            if s < steps_l:
                fw_l[s][h].wait_recv()
                if s + 1 < steps_l:
                    fw_l[s + 1][h].start()
        grad = grad + term(wrap(z - 1 - s), ag_r.at[s])
        if s < steps_l:
            grad = grad + term(wrap(z + 1 + s), ag_l.at[s])
        for number in plan_s.get(s, ()):
            itself.stage(number)

    own_g, rq, gy, go = r["own_g"], r["g_rq"], r["g_y"], r["g_o"]
    rows_g = own_g.shape[1]
    for j in range(nq):
        own_g[j] = grad[j * rows_g : (j + 1) * rows_g]
    first = group_q.copies((r["g_s0"], r["g_r0"]), lambda p: own_g.at[p], lambda o: rq.at[o - 1])
    for copy in first:
        copy.start()
    for number in plan_s.get("a", ()):
        itself.stage(number)
    total = own_g[q]
    for o in range(nq - 1):
        first[o].wait_recv()
        total = total + rq[o]
    gy[y] = total
    second = group_y.copies((r["g_s1"], r["g_r1"]), lambda p: gy.at[y], lambda o: gy.at[y])
    for copy in second:
        copy.start()
    for number in plan_s.get("b", ()):
        itself.stage(number)
    for copy in second:
        copy.wait_recv()
    total = gy[0]
    for j in range(1, ny):
        total = total + gy[j]
    go[q] = total
    third = group_q.copies((r["g_s2"], r["g_r2"]), lambda p: go.at[q], lambda o: go.at[q])
    for copy in third:
        copy.start()
    neigh.stage(6)
    itself.stage(6)
    for copy in third:
        copy.wait_recv()
    for j in range(nq):
        r["g1"][j * rows_g : (j + 1) * rows_g, :] = go[j]
    for copies in rs_r + rs_l + fw_r + fw_l + [first, second, third]:
        for copy in copies:
            copy.wait_send()


TOTAL_NAMES = ("rxc", "vy", "ry", "va", "vb", "fy", "fo") + tuple(
    f"{kind}{i}" for i in range(6) for kind in ("s", "r")
)
NEIGH_PLAN = {16: {3: (1,), 4: (2,), 5: (3,), 6: (4,), 7: (5,)}, 4: {1: (1, 2, 3), "mid": (4, 5)}}
SELF_PLAN = {16: {2: (1,), 3: (2,), 4: (3,), 5: (4,), 6: (5,)}, 4: {0: (1,), 1: (2, 3), "a": (4,), "b": (5,)}}


def exchange(mesh_shape, x, xt, agg2, w, og, w2s, w2n):
    nz, ny, nq, zblock = mesh_shape
    targets, width = og.shape
    half = targets // 2
    rows_q, rows_y, rows_g = width // nq, width // nq // ny, x.shape[1] // nq
    steps_r, steps_l = nz // 2, nz // 2 - 1
    V, D = pltpu.VMEM, pltpu.SemaphoreType.DMA
    scratch = dict(
        part=V((nz, targets, width), F32),
        out_r=V((steps_r, 2, half, width), BF16),
        out_l=V((steps_l, 2, half, width), BF16),
        in_r=V((steps_r, 2, half, width), BF16),
        in_l=V((steps_l, 2, half, width), BF16),
        ag_r=V((steps_r, 2, half, width), BF16),
        ag_l=V((steps_l, 2, half, width), BF16),
        pg=V((2, half, width), BF16),
        hid=V((targets, width), BF16),
        back=V((targets, width), F32),
        own_n=V((nq, rows_q, width), F32),
        own_s=V((nq, rows_q, width), F32),
        own_g=V((nq, rows_g, width), F32),
        g_rq=V((nq - 1, rows_g, width), F32),
        g_y=V((ny, rows_g, width), F32),
        g_o=V((nq, rows_g, width), F32),
    )
    for i, size in enumerate((nq - 1, ny - 1, nq - 1)):
        scratch[f"g_s{i}"] = D((size,))
        scratch[f"g_r{i}"] = D((size,))
    for name in ("rs_r", "rs_l", "ag_r", "ag_l"):
        steps = steps_r if name.endswith("r") else steps_l
        scratch[name + "s"] = D((steps, 2))
        scratch[name + "r"] = D((steps, 2))
    for lead in ("n_", "s_"):
        scratch[lead + "rxc"] = V((nq - 1, rows_q, width), F32)
        scratch[lead + "vy"] = V((ny, rows_y, width), F32)
        scratch[lead + "ry"] = V((ny - 1, rows_y, width), F32)
        scratch[lead + "va"] = V((zblock, rows_y, width), F32)
        scratch[lead + "vb"] = V((nz // zblock, rows_y, width), F32)
        scratch[lead + "fy"] = V((ny, rows_y, width), F32)
        scratch[lead + "fo"] = V((nq, ny, rows_y, width), F32)
        for i, size in enumerate((nq, ny, zblock, nz // zblock, ny, nq)):
            scratch[lead + f"s{i}"] = D((size - 1,))
            scratch[lead + f"r{i}"] = D((size - 1,))
    names = ("x", "xt", "agg2", "w", "og", "w2s", "w2n", "logits", "g1", "gs", "gn") + tuple(scratch)
    vmem = pl.BlockSpec(memory_space=pltpu.VMEM)
    return pl.pallas_call(
        functools.partial(exchange_kernel, mesh_shape, names),
        out_shape=(
            jax.ShapeDtypeStruct((targets, width), BF16),
            jax.ShapeDtypeStruct((x.shape[1], width), F32),
            jax.ShapeDtypeStruct((width, width), F32),
            jax.ShapeDtypeStruct((width, width), F32),
        ),
        in_specs=[vmem] * 7,
        out_specs=(vmem,) * 4,
        scratch_shapes=list(scratch.values()),
        compiler_params=pltpu.CompilerParams(
            collective_id=0, has_side_effects=True, vmem_limit_bytes=32 << 20
        ),
    )(x, xt, agg2, w, og, w2s, w2n)


def hand_out_kernel(logits, g1, gs, gn, o0, o1, o2, o3, o4):
    width = o1.shape[0]
    o0[...] = logits[...]
    o1[...] = g1[0:width, :]
    o2[...] = g1[width:, :]
    o3[...] = gs[...]
    o4[...] = gn[...]


def hand_out(logits, g1, gs, gn):
    vmem = pl.BlockSpec(memory_space=pltpu.VMEM)
    like = lambda a: jax.ShapeDtypeStruct(a.shape, a.dtype)
    piece = jax.ShapeDtypeStruct((g1.shape[0] // 2, g1.shape[1]), F32)
    return pl.pallas_call(
        hand_out_kernel,
        out_shape=(like(logits), piece, piece, like(gs), like(gn)),
        in_specs=[vmem] * 4,
        out_specs=(vmem,) * 5,
        compiler_params=pltpu.CompilerParams(vmem_limit_bytes=8 << 20),
    )(logits, g1, gs, gn)


def local(shape, tx, frontier, n1, c1, w1s, w1n, history, n2, c2, w2s, w2n, og):
    x, xt, agg2 = gather_means(tx, frontier, n1, c1, history, n2, c2)
    w = jnp.concatenate([w1s, w1n], axis=0)
    return hand_out(*exchange(shape, x, xt, agg2, w, og, w2s, w2n))


SPECS = (
    P("feat", "dp"),
    P("feat", "dp"),
    P(None, "dp"),
    P("dp"),
    P("feat", None),
    P("feat", None),
    P(("dp", "feat"), None),
    P(None, ("dp", "feat")),
    P(("dp", "feat")),
    P(),
    P(),
    P(("dp", "feat"), None),
)


def build(mesh, shape):
    return jax.shard_map(
        functools.partial(local, shape),
        mesh=mesh,
        in_specs=SPECS,
        out_specs=(P(("dp", "feat"), None), P("feat", None), P("feat", None), P(), P()),
        check_vma=False,
    )


def solution(mesh):
    return build(mesh, (mesh.shape["feat"], mesh.shape["dp"] // 8, 8, 4))
```

time: 957 us -> 135 us (0.14)
  waiting for transfers between devices: 831 us -> 0 us
  Pallas kernels: 0 us -> 130 us
  local copies, waits for them, and re-layouts: 90.4 us -> 1.85 us
  between operations: 14 us -> 0.74 us
  matrix products: 11.2 us -> 0 us
    psum x2 -> x0, waiting for transfers between devices: 694 us -> none  [the longest x1 486 us: local(): lax.psum((contract_rows(hidden, out_grad), contract_rows(agg_two, out_gra...]
    pallas_call x0 -> x3, Pallas kernels: none -> 130 us  [the longest x1 106 us: exchange(): pl.pallas_call(functools.partial(exchange_kernel, mesh_shape, names), out...]
    gather x2 -> x0, local copies, waits for them, and re-layouts: 82.1 us -> none  [the longest x1 72.2 us: mean_columns(): picked = lookup[:, col_ids]]
    reduce_scatter x1 -> x0, waiting for transfers between devices: 75.6 us -> none  [local(): lax.psum_scatter(contract_rows(self_cols, w1_self) + contract_rows(neigh_...]
    all_gather x1 -> x0, waiting for transfers between devices: 61.4 us -> none  [local(): grad_piece = lax.all_gather(pre_grad, 'feat', axis=0, tiled=True)]
    dot_general x9 -> x0, matrix products: 11.2 us -> none  [the longest x4 4.14 us: contract_rows(): lax.dot_general(left, right, (((0,), (0,)), ((), ())), preferred_element_...]
  transfers between devices with their start and end apart: 4 -> 0, of which waited for: 4 -> 0; matrix products, arithmetic and copies ran while one was open for 2% -> 0% of each run, Pallas kernels for 0% -> 0%
where the time goes in v1:
time: 135 us; the launch traced here: 134 us
  Pallas kernels  130 us (96%)
  local copies, waits for them, and re-layouts  1.85 us (1%)
  other arithmetic  1.79 us (1%)
    pallas_call x1, Pallas kernels, exchange(): pl.pallas_call(functools.partial(exchange_kernel, mesh_shape, names), out...  106 us
    pallas_call x1, Pallas kernels, gather_means(): pl.pallas_call(functools.partial(gather_kernel, slots, 32), out_shape=(ja...  23.1 us

profile of v1, /device:TPU:1, one launch (start us, length us, event | category | flops | bytes accessed | tf_op | source)
XLA Modules:
  0.0 134.3 jit_solution(8842007942306101225)
XLA Ops:
  0.6 0.0 copy-start.6
  0.6 0.0 copy-start.2
  0.7 0.8 pad_maximum_fusion.refs_3_
  1.5 0.0 copy-done.6
  1.5 0.0 copy-start.1
  1.5 1.0 fusion
  2.5 0.0 copy-start.7
  2.5 0.0 copy-start.8
  2.5 0.0 copy-done.2
  2.5 0.0 copy-done.1
  2.5 0.7 copy-done.7
  3.2 0.0 copy-done.8
  3.2 0.0 copy-start
  3.2 1.1 copy-done
  4.3 0.0 copy-start.3
  4.3 0.0 copy-start.4
  4.3 0.0 copy-start.5
  4.3 23.1 %shard_map.155 = (bf16[16,128,128]{2,1,0:T(8,128)(2,1)S(1)}, bf16[16,128,128]{2,1,0:T(8,128)(2,1)S(1)}, bf16[128,256]{1,0:T(8,128)(2,1)S(1)}) custom-call(s32[20480]{0:T(1024)S(1)} %reshape.18.idx_ref, s32[1,2048]{1,0:T(1,128)S(1)} %bitcast.2, bf16[64,6144]{1,0:T(8,128)(2,1)S(1)} %copy-done, bf16[64,2048]{1,0:T(8,128)(2,1)S(1)} %copy-done.1, ...), custom_call_target="tpu_custom_call" | custom-call | tf_op jit(solution)/shard_map/pallas_call | solution.py:76
  27.5 0.0 copy-done.3
  27.5 0.0 copy-done.4
  27.5 0.0 copy-done.5
  27.5 105.9 %shard_map.156 = (bf16[128,256]{1,0:T(8,128)(2,1)S(1)}, f32[128,256]{1,0:T(8,128)S(1)}, f32[256,256]{1,0:T(8,128)S(1)}, f32[256,256]{1,0:T(8,128)S(1)}) custom-call(bf16[16,128,128]{2,1,0:T(8,128)(2,1)S(1)} %get-tuple-element.12.refs_0_, bf16[16,128,128]{2,1,0:T(8,128)(2,1)S(1)} %get-tuple-element.13.refs_1_, ...), custom_call_target="tpu_custom_call" | custom-call | tf_op jit(solution)/shard_map/pallas_call | solution.py:415
  133.4 0.9 shard_map.157
  (1 shorter events, 0.0 us)
Async XLA Ops:
  0.6 0.8 copy-start.6
  0.6 1.9 %copy-start.2 = (bf16[512,256]{1,0:T(8,128)(2,1)S(1)}, bf16[512,256]{1,0:T(8,128)(2,1)}, u32[]{:S(2)}) copy-start(bf16[512,256]{1,0:T(8,128)(2,1)} %hist_ref.1) | copy-start | bytes 786436
  1.5 1.0 copy-start.1
  2.5 0.7 copy-start.7
  2.5 0.7 copy-start.8
  3.2 1.1 copy-start
  4.3 23.1 %copy-start.3 = (bf16[256,256]{1,0:T(8,128)(2,1)S(1)}, bf16[256,256]{1,0:T(8,128)(2,1)}, u32[]{:S(2)}) copy-start(bf16[256,256]{1,0:T(8,128)(2,1)} %refs_5_.1) | copy-start | bytes 393220
  4.3 23.1 %copy-start.4 = (bf16[256,256]{1,0:T(8,128)(2,1)S(1)}, bf16[256,256]{1,0:T(8,128)(2,1)}, u32[]{:S(2)}) copy-start(bf16[256,256]{1,0:T(8,128)(2,1)} %refs_6_.1) | copy-start | bytes 393220
  4.3 23.2 %copy-start.5 = (bf16[128,256]{1,0:T(8,128)(2,1)S(1)}, bf16[128,256]{1,0:T(8,128)(2,1)}, u32[]{:S(2)}) copy-start(bf16[128,256]{1,0:T(8,128)(2,1)} %refs_4_.1) | copy-start | bytes 196612

commit v2 on v1

v2 whole, which is shorter than its diff:
```python
import functools

import jax
import jax.numpy as jnp
from jax import lax
from jax.experimental import pallas as pl
from jax.experimental.pallas import tpu as pltpu
from jax.sharding import PartitionSpec as P

MESH = pl.DeviceIdType.MESH
F32, BF16 = jnp.float32, jnp.bfloat16


def dot(left, right):
    return jnp.dot(left, right, preferred_element_type=F32)


def dot_rows(left, right):
    return lax.dot_general(left, right, (((0,), (0,)), ((), ())), preferred_element_type=F32)


class Spread:
    def __init__(self, size, mine, device):
        self.size, self.mine, self.device = size, mine, device

    def peer(self, offset):
        return lax.rem(self.mine + offset, self.size)

    def copies(self, sems, source, target):
        send, recv = sems
        return [
            pltpu.make_async_remote_copy(
                src_ref=source(self.peer(o)),
                dst_ref=target(o),
                send_sem=send.at[o - 1],
                recv_sem=recv.at[o - 1],
                device_id=self.device(self.peer(o)),
                device_id_type=MESH,
            )
            for o in range(1, self.size)
        ]

    def greet(self, barrier):
        for o in range(1, self.size):
            pl.semaphore_signal(
                barrier, inc=1, device_id=self.device(self.peer(o)), device_id_type=MESH
            )


class Total:
    def __init__(self, groups, refs, own, out):
        self.xc, self.y, self.z = groups
        (self.rxc, self.vy, self.ry, self.vz, self.fy, self.fo) = refs[:6]
        sems = refs[6:]
        self.sems = [(sems[2 * i], sems[2 * i + 1]) for i in range(5)]
        self.own, self.out = own, out

    def copies(self, number):
        sems = self.sems[number]
        if number == 0:
            return self.xc.copies(sems, lambda p: self.own.at[p], lambda o: self.rxc.at[o - 1])
        if number == 1:
            return self.y.copies(sems, lambda p: self.vy.at[p], lambda o: self.ry.at[o - 1])
        if number == 2:
            me = self.z.mine
            return self.z.copies(sems, lambda p: self.vz.at[me], lambda o: self.vz.at[me])
        if number == 3:
            me = self.y.mine
            return self.y.copies(sems, lambda p: self.fy.at[me], lambda o: self.fy.at[me])
        me = self.xc.mine
        return self.xc.copies(sems, lambda p: self.fy, lambda o: self.fo.at[me])

    def stage(self, number):
        if number > 0:
            for copy in self.copies(number - 1):
                copy.wait_recv()
        if number == 1:
            total = self.own[self.xc.mine]
            for o in range(self.xc.size - 1):
                total = total + self.rxc[o]
            part = self.vy.shape[1]
            for j in range(self.y.size):
                self.vy[j] = total[j * part : (j + 1) * part]
        elif number == 2:
            total = self.vy[self.y.mine]
            for o in range(self.y.size - 1):
                total = total + self.ry[o]
            self.vz[self.z.mine] = total
        elif number == 3:
            total = self.vz[0]
            for j in range(1, self.z.size):
                total = total + self.vz[j]
            self.fy[self.y.mine] = total
        elif number == 4:
            self.fo[self.xc.mine] = self.fy[...]
        elif number == 5:
            part = self.fo.shape[2]
            for q in range(self.xc.size):
                for j in range(self.y.size):
                    at = (q * self.y.size + j) * part
                    self.out[at : at + part, :] = self.fo[q, j]
            for done in range(5):
                for copy in self.copies(done):
                    copy.wait_send()
        if number < 5:
            for copy in self.copies(number):
                copy.start()


class Chain:
    def __init__(self, steps, arrived, sems, source, device):
        self.steps, self.arrived, self.sems = steps, arrived, sems
        self.source, self.device = source, device

    def copy(self, s, h):
        return pltpu.make_async_remote_copy(
            src_ref=self.source(s).at[h],
            dst_ref=self.arrived.at[s, h],
            send_sem=self.sems[0].at[s, h],
            recv_sem=self.sems[1].at[s, h],
            device_id=self.device(s),
            device_id_type=MESH,
        )

    def start(self, s, h):
        if s < self.steps:
            self.copy(s, h).start()

    def wait_recv(self, s, h):
        self.copy(s, h).wait_recv()

    def finish(self):
        for s in range(self.steps):
            for h in range(2):
                self.copy(s, h).wait_send()


UNROLL = 16


def step_kernel(shape, names, *refs):
    nz, ny, nq = shape
    r = dict(zip(names, refs))
    z = lax.axis_index("feat")
    dp = lax.axis_index("dp")
    q, y = lax.rem(dp, nq), lax.div(dp, nq)
    wrap = lambda v: lax.rem(v + 2 * nz, nz)

    group_q = Spread(nq, q, lambda p: (z, y * nq + p))
    group_y = Spread(ny, y, lambda p: (z, p * nq + q))
    group_z = Spread(nz, z, lambda p: (p, dp))
    groups = (group_q, group_y, group_z)
    barrier = pltpu.get_barrier_semaphore()
    for group in groups:
        group.greet(barrier)

    x, w, part, og, agg2 = r["x"], r["w"], r["part"], r["og"], r["agg2"]
    f_ref, tab, rows, idx_ref = r["f"], r["tab"], r["rows"], r["idx"]
    width, nodes = f_ref.shape
    targets = r["tx"].shape[1]
    slots = idx_ref.shape[0] // targets
    half = og.shape[0] // 2
    w[0:width, :] = r["w1s"][...]
    w[width:, :] = r["w1n"][...]
    tab[nodes : nodes + 8, :] = jnp.zeros((8, 128), F32)

    def turn(i, carry):
        at = pl.multiple_of(i * 256, 256)
        for j in range(2):
            tab[pl.ds(at + j * 128, 128), 0:width] = f_ref[:, pl.ds(at + j * 128, 128)].astype(F32).T
        return carry

    lax.fori_loop(0, nodes // 256, turn, 0)

    c2 = r["c2"][...]
    node = lax.broadcasted_iota(jnp.int32, (r["hist"].shape[0], c2.shape[1]), 0)
    times = jnp.zeros(node.shape, F32)
    for k in range(r["n2"].shape[0]):
        live = jnp.where(k < c2, r["n2"][k : k + 1, :], -1)
        times = times + jnp.where(node == live, 1.0, 0.0)
    total = dot_rows(r["hist"][...], times.astype(BF16))
    agg2[...] = (total / c2.astype(F32)).T.astype(BF16)

    own_n, own_s = r["own_n"], r["own_s"]
    rows_q = own_n.shape[1]

    def store_own(own, value):
        for j in range(nq):
            own[j] = value[j * rows_q : (j + 1) * rows_q]

    store_own(own_n, dot_rows(agg2[...], og[...]))
    neigh = Total(groups, [r["n_" + n] for n in TOTAL_NAMES], own_n, r["gn"])
    itself = Total(groups, [r["s_" + n] for n in TOTAL_NAMES], own_s, r["gs"])

    def gather(c):
        base = c * 128

        def pick(i, carry):
            for u in range(UNROLL):
                t = base + i * UNROLL + u
                terms = [tab[pl.ds(idx_ref[k * targets + t], 1), :] for k in range(slots)]
                while len(terms) > 1:
                    odd = terms[-1:] if len(terms) % 2 else []
                    terms = [a + b for a, b in zip(terms[::2], terms[1::2])] + odd
                rows[pl.ds(i * UNROLL + u, 1), :] = terms[0]
            return carry

        lax.fori_loop(0, 128 // UNROLL, pick, 0)
        at = pl.multiple_of(base, 128)
        mean = rows[...].T[0:width, :] / r["cnt"][:, pl.ds(at, 128)].astype(F32)
        both = jnp.concatenate([r["tx"][:, pl.ds(at, 128)].astype(F32), mean], axis=0)
        x[c] = both.astype(BF16)
        part[c] = dot(both.T.astype(BF16), w[...])

    jump = nz // 4
    reach_r, reach_l = nz // 2, nz // 2 - 1
    far_r, far_l, near = reach_r - jump + 1, reach_l - jump + 1, jump - 1
    to = lambda offset: (wrap(z + offset), dp)

    def sums(name, steps, sign, far):
        out = r["out_" + name]
        device = lambda s: to(sign * (jump if far and s == steps - 1 else 1))
        return Chain(steps, r["in_" + name], (r["rs_s" + name], r["rs_r" + name]), lambda s: out.at[s], device)

    red_rf, red_lf = sums("rf", far_r, 1, True), sums("lf", far_l, -1, True)
    red_rn, red_ln = sums("rn", near, 1, False), sums("ln", near, -1, False)

    def send_sums(name, chain, s, c):
        for h in range(2):
            value = part[c, h * half : (h + 1) * half, :]
            if s > 0:
                chain.wait_recv(s - 1, h)
                value = value + chain.arrived[s - 1, h].astype(F32)
            r["out_" + name][s, h] = value.astype(BF16)
            chain.start(s, h)

    plan = [("f", 0)]
    for s in range(near):
        plan += [("n", s), ("f", s + 1)]
    plan += [("f", s) for s in range(near + 1, far_r)]
    offsets_r = [reach_r - s if kind == "f" else near - s for kind, s in plan]
    offsets_l = [0 if kind == "f" and s == far_l else (s - reach_l if kind == "f" else s - near) for kind, s in plan]

    def select(i, values):
        chosen = jnp.int32(values[0])
        for j in range(1, len(values)):
            chosen = jnp.where(i == j, values[j], chosen)
        return chosen

    def advance(i, carry):
        gather(wrap(z + select(i, offsets_r)))
        gather(wrap(z + select(i, offsets_l)))
        for j, (kind, s) in enumerate(plan):

            @pl.when(i == j)
            def _():
                if j == 0:
                    pl.semaphore_wait(barrier, sum(group.size - 1 for group in groups))
                if kind == "f":
                    send_sums("rf", red_rf, s, wrap(z + reach_r - s))
                    if s < far_l:
                        send_sums("lf", red_lf, s, wrap(z - reach_l + s))
                else:
                    send_sums("rn", red_rn, s, wrap(z + near - s))
                    send_sums("ln", red_ln, s, wrap(z - near + s))
                for number in NEIGH_PLAN[nz].get(j, ()):
                    neigh.stage(number)

        return carry

    lax.fori_loop(0, len(plan), advance, 0)

    r["back"][...] = lax.dot_general(
        og[...], r["w2s"][...], (((1,), (1,)), ((), ())), preferred_element_type=F32
    )
    later = dot(agg2[...], r["w2n"][...])

    pg, hid = r["pg"], r["hid"]

    def blocks(name, steps, sign, far):
        device = lambda s: to(sign * (jump if far and s == 0 else 1))
        arrived = r["ag_" + name]
        source = lambda s: pg if s == 0 else arrived.at[s - 1]
        return Chain(steps, arrived, (r["ag_s" + name], r["ag_r" + name]), source, device)

    all_rf, all_lf = blocks("rf", far_r, 1, True), blocks("lf", far_l, -1, True)
    all_rn, all_ln = blocks("rn", near, 1, False), blocks("ln", near, -1, False)

    for h in range(2):
        span = slice(h * half, (h + 1) * half)
        pre = part[z, span, :]
        for chain in (red_rf, red_lf, red_rn, red_ln):
            if chain.steps:
                chain.wait_recv(chain.steps - 1, h)
                pre = pre + chain.arrived[chain.steps - 1, h].astype(F32)
        sig = 1.0 / (1.0 + jnp.exp(-pre))
        pg[h] = (r["back"][span, :] * (sig * (1.0 + pre * (1.0 - sig)))).astype(BF16)
        for chain in (all_rf, all_lf, all_rn, all_ln):
            chain.start(0, h)
        hid[span, :] = (pre * sig).astype(BF16)

    store_own(own_s, dot_rows(hid[...], og[...]))
    itself.stage(0)
    r["logits"][...] = (dot(hid[...], r["w2s"][...]) + later).astype(BF16)

    def term(c, block):
        return dot(x[c], jnp.concatenate([block[0], block[1]], axis=0))

    grad = term(z, pg)
    order = [("n", 0)] if near else []
    for s in range(far_r):
        order += [("f", s)] + ([("n", s + 1)] if s + 1 < near else [])
    for j, (kind, s) in enumerate(order):
        pair = ((all_rf, -jump - s), (all_lf, jump + s)) if kind == "f" else ((all_rn, -1 - s), (all_ln, 1 + s))
        pair = [(chain, offset) for chain, offset in pair if s < chain.steps]
        for h in range(2):
            for chain, offset in pair:
                chain.wait_recv(s, h)
                chain.start(s + 1, h)
        for chain, offset in pair:
            grad = grad + term(wrap(z + offset), chain.arrived.at[s])
        for number in AFTER_NEIGH_PLAN[nz].get(j, ()):
            neigh.stage(number)
        for number in SELF_PLAN[nz].get(j, ()):
            itself.stage(number)

    own_g, rq, gy, go = r["own_g"], r["g_rq"], r["g_y"], r["g_o"]
    rows_g = own_g.shape[1]
    for j in range(nq):
        own_g[j] = grad[j * rows_g : (j + 1) * rows_g]
    first = group_q.copies((r["g_s0"], r["g_r0"]), lambda p: own_g.at[p], lambda o: rq.at[o - 1])
    for copy in first:
        copy.start()
    for number in SELF_PLAN[nz].get("a", ()):
        itself.stage(number)
    total = own_g[q]
    for o in range(nq - 1):
        first[o].wait_recv()
        total = total + rq[o]
    gy[y] = total
    second = group_y.copies((r["g_s1"], r["g_r1"]), lambda p: gy.at[y], lambda o: gy.at[y])
    for copy in second:
        copy.start()
    for number in SELF_PLAN[nz].get("b", ()):
        itself.stage(number)
    for chain in (red_rf, red_lf, red_rn, red_ln, all_rf, all_lf, all_rn, all_ln):
        chain.finish()
    neigh.stage(5)
    for copy in second:
        copy.wait_recv()
    total = gy[0]
    for j in range(1, ny):
        total = total + gy[j]
    go[q] = total
    third = group_q.copies((r["g_s2"], r["g_r2"]), lambda p: go.at[q], lambda o: go.at[q])
    for copy in third:
        copy.start()
    for number in SELF_PLAN[nz].get("c", ()):
        itself.stage(number)
    itself.stage(5)
    for copy in third:
        copy.wait_recv()
    for j in range(nq):
        r["g1"][j * rows_g : (j + 1) * rows_g, :] = go[j]
    for copies in (first, second, third):
        for copy in copies:
            copy.wait_send()


TOTAL_NAMES = ("rxc", "vy", "ry", "vz", "fy", "fo") + tuple(
    f"{kind}{i}" for i in range(5) for kind in ("s", "r")
)
NEIGH_PLAN = {16: {0: (0,), 3: (1,), 6: (2,)}, 8: {0: (0,), 2: (1,)}}
AFTER_NEIGH_PLAN = {16: {2: (3,), 5: (4,)}, 8: {0: (2,), 1: (3,), 2: (4,)}}
SELF_PLAN = {
    16: {3: (1,), 6: (2,), "b": (3,), "c": (4,)},
    8: {0: (1,), 1: (2,), "b": (3,), "c": (4,)},
}


def step(shape, idx, cnt, f, tx, hist, n2, c2, w1s, w1n, og, w2s, w2n):
    nz, ny, nq = shape
    targets, width = og.shape
    half = targets // 2
    deep = 2 * tx.shape[0]
    rows_q, rows_y, rows_g = width // nq, width // nq // ny, deep // nq
    jump = nz // 4
    lengths = dict(rf=nz // 2 - jump + 1, lf=nz // 2 - jump, rn=jump - 1, ln=jump - 1)
    V, D = pltpu.VMEM, pltpu.SemaphoreType.DMA
    scratch = dict(
        tab=V((f.shape[1] + 8, 128), F32),
        rows=V((128, 128), F32),
        x=V((nz, deep, 128), BF16),
        w=V((deep, width), BF16),
        agg2=V((targets, width), BF16),
        part=V((nz, targets, width), F32),
        pg=V((2, half, width), BF16),
        hid=V((targets, width), BF16),
        back=V((targets, width), F32),
        own_n=V((nq, rows_q, width), F32),
        own_s=V((nq, rows_q, width), F32),
        own_g=V((nq, rows_g, width), F32),
        g_rq=V((nq - 1, rows_g, width), F32),
        g_y=V((ny, rows_g, width), F32),
        g_o=V((nq, rows_g, width), F32),
    )
    for i, size in enumerate((nq - 1, ny - 1, nq - 1)):
        scratch[f"g_s{i}"] = D((size,))
        scratch[f"g_r{i}"] = D((size,))
    for name, steps in lengths.items():
        for lead in ("out_", "in_", "ag_"):
            scratch[lead + name] = V((steps, 2, half, width), BF16)
        for lead in ("rs_s", "rs_r", "ag_s", "ag_r"):
            scratch[lead + name] = D((steps, 2))
    for lead in ("n_", "s_"):
        scratch[lead + "rxc"] = V((nq - 1, rows_q, width), F32)
        scratch[lead + "vy"] = V((ny, rows_y, width), F32)
        scratch[lead + "ry"] = V((ny - 1, rows_y, width), F32)
        scratch[lead + "vz"] = V((nz, rows_y, width), F32)
        scratch[lead + "fy"] = V((ny, rows_y, width), F32)
        scratch[lead + "fo"] = V((nq, ny, rows_y, width), F32)
        for i, size in enumerate((nq, ny, nz, ny, nq)):
            scratch[lead + f"s{i}"] = D((size - 1,))
            scratch[lead + f"r{i}"] = D((size - 1,))
    inputs = ("idx", "cnt", "f", "tx", "hist", "n2", "c2", "w1s", "w1n", "og", "w2s", "w2n")
    names = inputs + ("logits", "g1", "gs", "gn") + tuple(scratch)
    vmem = pl.BlockSpec(memory_space=pltpu.VMEM)
    return pl.pallas_call(
        functools.partial(step_kernel, shape, names),
        out_shape=(
            jax.ShapeDtypeStruct((targets, width), BF16),
            jax.ShapeDtypeStruct((deep, width), F32),
            jax.ShapeDtypeStruct((width, width), F32),
            jax.ShapeDtypeStruct((width, width), F32),
        ),
        in_specs=[pl.BlockSpec(memory_space=pltpu.SMEM)] + [vmem] * (len(inputs) - 1),
        out_specs=(vmem,) * 4,
        scratch_shapes=list(scratch.values()),
        compiler_params=pltpu.CompilerParams(
            collective_id=0, has_side_effects=True, vmem_limit_bytes=40 << 20
        ),
    )(idx, cnt, f, tx, hist, n2, c2, w1s, w1n, og, w2s, w2n)


def hand_out_kernel(logits, g1, gs, gn, o0, o1, o2, o3, o4):
    width = o1.shape[0]
    o0[...] = logits[...]
    o1[...] = g1[0:width, :]
    o2[...] = g1[width:, :]
    o3[...] = gs[...]
    o4[...] = gn[...]


def hand_out(logits, g1, gs, gn):
    vmem = pl.BlockSpec(memory_space=pltpu.VMEM)
    like = lambda a: jax.ShapeDtypeStruct(a.shape, a.dtype)
    piece = jax.ShapeDtypeStruct((g1.shape[0] // 2, g1.shape[1]), F32)
    return pl.pallas_call(
        hand_out_kernel,
        out_shape=(like(logits), piece, piece, like(gs), like(gn)),
        in_specs=[vmem] * 4,
        out_specs=(vmem,) * 5,
        compiler_params=pltpu.CompilerParams(vmem_limit_bytes=8 << 20),
    )(logits, g1, gs, gn)


def local(shape, tx, frontier, n1, c1, w1s, w1n, history, n2, c2, w2s, w2n, og):
    live = lax.broadcasted_iota(jnp.int32, n1.shape, 0) < c1[None, :]
    idx = jnp.where(live, n1, frontier.shape[1]).reshape(-1)
    return hand_out(
        *step(
            shape, idx, c1.reshape(1, -1), frontier, tx, history, n2, c2.reshape(1, -1),
            w1s, w1n, og, w2s, w2n,
        )
    )


SPECS = (
    P("feat", "dp"),
    P("feat", "dp"),
    P(None, "dp"),
    P("dp"),
    P("feat", None),
    P("feat", None),
    P(("dp", "feat"), None),
    P(None, ("dp", "feat")),
    P(("dp", "feat")),
    P(),
    P(),
    P(("dp", "feat"), None),
)


def build(mesh, shape):
    return jax.shard_map(
        functools.partial(local, shape),
        mesh=mesh,
        in_specs=SPECS,
        out_specs=(P(("dp", "feat"), None), P("feat", None), P("feat", None), P(), P()),
        check_vma=False,
    )


def solution(mesh):
    return build(mesh, (mesh.shape["feat"], mesh.shape["dp"] // 8, 8))
```

time: 135 us -> 107 us (0.79)
  Pallas kernels: 130 us -> 99.6 us
  local copies, waits for them, and re-layouts: 1.85 us -> 5.37 us
    pallas_call x2 -> x1, Pallas kernels: 129 us -> 98.7 us  [step(): pl.pallas_call(functools.partial(step_kernel, shape, names), out_shape=(j...]
    unnamed x18 -> x22, local copies, waits for them, and re-layouts: 1.83 us -> 5.35 us
where the time goes in v2:
time: 107 us
  Pallas kernels  99.6 us (93%)
  local copies, waits for them, and re-layouts  5.37 us (5%)
    pallas_call x1, Pallas kernels, step(): pl.pallas_call(functools.partial(step_kernel, shape, names), out_shape=(j...  98.7 us
    unnamed x22, local copies, waits for them, and re-layouts  5.35 us

profile of v2, /device:TPU:1, one launch (start us, length us, event | category | flops | bytes accessed | tf_op | source)
XLA Modules:
  0.0 106.7 jit_solution(11986083284647544535)
XLA Ops:
  0.6 0.0 copy-start.1
  0.6 0.0 copy-start.9
  0.7 1.0 fusion
  1.6 0.0 copy-start.3
  1.6 0.0 copy-start.5
  1.6 0.0 copy-start.8
  1.7 0.0 copy-start.10
  1.7 0.0 copy-done.1
  1.7 0.0 copy-done.9
  1.7 0.8 copy-done.3
  2.5 0.0 copy-done.5
  2.5 0.0 copy-done.8
  2.5 0.0 copy-done.10
  2.5 0.0 copy-start
  2.5 1.1 %copy-done = bf16[64,6144]{1,0:T(8,128)(2,1)S(1)} copy-done((bf16[64,6144]{1,0:T(8,128)(2,1)S(1)}, bf16[64,6144]{1,0:T(8,128)(2,1)}, u32[]{:S(2)}) %copy-start) | copy-done | bytes 786456
  3.7 0.0 copy-start.2
  3.7 0.9 copy-done.2
  4.6 0.0 copy-start.4
  4.6 0.9 copy-done.4
  5.5 0.0 copy-start.6
  5.5 0.8 copy-done.6
  6.3 0.0 copy-start.7
  6.3 0.8 copy-done.7
  7.0 98.7 %shard_map.155 = (bf16[128,256]{1,0:T(8,128)(2,1)S(1)}, f32[128,256]{1,0:T(8,128)S(1)}, f32[256,256]{1,0:T(8,128)S(1)}, f32[256,256]{1,0:T(8,128)S(1)}) custom-call(s32[20480]{0:T(1024)S(1)} %reshape.18.refs_0_, s32[1,2048]{1,0:T(1,128)S(1)} %bitcast.2, bf16[64,6144]{1,0:T(8,128)(2,1)S(1)} %copy-done, bf16[64,2048]{1,0:T(8,128)(2,1)S(1)} %copy-done.1, ...), custom_call_target="tpu_custom_call" | custom-call | tf_op jit(solution)/shard_map/pallas_call | solution.py:428
  105.8 0.9 shard_map.156
  (1 shorter events, 0.0 us)
Async XLA Ops:
  0.6 1.1 copy-start.1
  0.6 1.1 copy-start.9
  1.6 0.9 copy-start.3
  1.6 0.9 copy-start.5
  1.6 0.9 copy-start.8
  1.7 0.9 copy-start.10
  2.5 1.1 %copy-start = (bf16[64,6144]{1,0:T(8,128)(2,1)S(1)}, bf16[64,6144]{1,0:T(8,128)(2,1)}, u32[]{:S(2)}) copy-start(bf16[64,6144]{1,0:T(8,128)(2,1)} %refs_2_.1) | copy-start | bytes 2359300
  3.7 0.9 copy-start.2
  4.6 0.9 copy-start.4
  5.5 0.8 copy-start.6
  6.3 0.8 copy-start.7

commit v3 on v2

--- a/solution.py
+++ b/solution.py
@@ -141,6 +141,17 @@
 def step_kernel(shape, names, *refs):
     nz, ny, nq = shape
     r = dict(zip(names, refs))
+    loads = {
+        name: pltpu.make_async_copy(r[name], r["v_" + name], r["in_sem"].at[i])
+        for i, name in enumerate(INPUTS)
+    }
+    for load in loads.values():
+        load.start()
+
+    def take(*wanted):
+        for name in wanted:
+            loads[name].wait()
+
     z = lax.axis_index("feat")
     dp = lax.axis_index("dp")
     q, y = lax.rem(dp, nq), lax.div(dp, nq)
@@ -154,14 +165,14 @@
     for group in groups:
         group.greet(barrier)
 
+    r = {**r, **{name: r["v_" + name] for name in INPUTS}}
     x, w, part, og, agg2 = r["x"], r["w"], r["part"], r["og"], r["agg2"]
     f_ref, tab, rows, idx_ref = r["f"], r["tab"], r["rows"], r["idx"]
     width, nodes = f_ref.shape
     targets = r["tx"].shape[1]
+    take("f")
     slots = idx_ref.shape[0] // targets
-    half = og.shape[0] // 2
-    w[0:width, :] = r["w1s"][...]
-    w[width:, :] = r["w1n"][...]
+    half = og.shape[1] // 2
     tab[nodes : nodes + 8, :] = jnp.zeros((8, 128), F32)
 
     def turn(i, carry):
@@ -172,14 +183,9 @@
 
     lax.fori_loop(0, nodes // 256, turn, 0)
 
-    c2 = r["c2"][...]
-    node = lax.broadcasted_iota(jnp.int32, (r["hist"].shape[0], c2.shape[1]), 0)
-    times = jnp.zeros(node.shape, F32)
-    for k in range(r["n2"].shape[0]):
-        live = jnp.where(k < c2, r["n2"][k : k + 1, :], -1)
-        times = times + jnp.where(node == live, 1.0, 0.0)
-    total = dot_rows(r["hist"][...], times.astype(BF16))
-    agg2[...] = (total / c2.astype(F32)).T.astype(BF16)
+    take("w1s", "w1n", "idx", "cnt", "tx")
+    w[:, 0:width] = r["w1s"][...].astype(F32).T.astype(BF16)
+    w[:, width:] = r["w1n"][...].astype(F32).T.astype(BF16)
 
     own_n, own_s = r["own_n"], r["own_s"]
     rows_q = own_n.shape[1]
@@ -188,29 +194,31 @@
         for j in range(nq):
             own[j] = value[j * rows_q : (j + 1) * rows_q]
 
-    store_own(own_n, dot_rows(agg2[...], og[...]))
     neigh = Total(groups, [r["n_" + n] for n in TOTAL_NAMES], own_n, r["gn"])
     itself = Total(groups, [r["s_" + n] for n in TOTAL_NAMES], own_s, r["gs"])
 
-    def gather(c):
-        base = c * 128
-
-        def pick(i, carry):
-            for u in range(UNROLL):
-                t = base + i * UNROLL + u
-                terms = [tab[pl.ds(idx_ref[k * targets + t], 1), :] for k in range(slots)]
-                while len(terms) > 1:
-                    odd = terms[-1:] if len(terms) % 2 else []
-                    terms = [a + b for a, b in zip(terms[::2], terms[1::2])] + odd
-                rows[pl.ds(i * UNROLL + u, 1), :] = terms[0]
-            return carry
-
-        lax.fori_loop(0, 128 // UNROLL, pick, 0)
-        at = pl.multiple_of(base, 128)
-        mean = rows[...].T[0:width, :] / r["cnt"][:, pl.ds(at, 128)].astype(F32)
-        both = jnp.concatenate([r["tx"][:, pl.ds(at, 128)].astype(F32), mean], axis=0)
-        x[c] = both.astype(BF16)
-        part[c] = dot(both.T.astype(BF16), w[...])
+    def gather(chunks):
+        for place, c in enumerate(chunks):
+            base = c * 128
+
+            def pick(i, carry):
+                for u in range(UNROLL):
+                    t = base + i * UNROLL + u
+                    terms = [tab[pl.ds(idx_ref[k * targets + t], 1), :] for k in range(slots)]
+                    while len(terms) > 1:
+                        odd = terms[-1:] if len(terms) % 2 else []
+                        terms = [a + b for a, b in zip(terms[::2], terms[1::2])] + odd
+                    rows[place, pl.ds(i * UNROLL + u, 1), :] = terms[0]
+                return carry
+
+            lax.fori_loop(0, 128 // UNROLL, pick, 0)
+        for place, c in enumerate(chunks):
+            at = pl.multiple_of(c * 128, 128)
+            mean = rows[place].T[0:width, :] / r["cnt"][:, pl.ds(at, 128)].astype(F32)
+            x[c, 0:width] = r["tx"][:, pl.ds(at, 128)]
+            x[c, width:] = mean.astype(BF16)
+        for c in chunks:
+            part[c] = dot(w[...], x[c])
 
     jump = nz // 4
     reach_r, reach_l = nz // 2, nz // 2 - 1
@@ -248,8 +256,7 @@
         return chosen
 
     def advance(i, carry):
-        gather(wrap(z + select(i, offsets_r)))
-        gather(wrap(z + select(i, offsets_l)))
+        gather([wrap(z + select(i, offsets_r)), wrap(z + select(i, offsets_l))])
         for j, (kind, s) in enumerate(plan):
 
             @pl.when(i == j)
@@ -263,17 +270,26 @@
                 else:
                     send_sums("rn", red_rn, s, wrap(z + near - s))
                     send_sums("ln", red_ln, s, wrap(z - near + s))
-                for number in NEIGH_PLAN[nz].get(j, ()):
-                    neigh.stage(number)
-
         return carry
 
     lax.fori_loop(0, len(plan), advance, 0)
 
+    take("hist", "n2", "c2", "og", "w2s", "w2n")
+    c2 = r["c2"][...]
+    node = lax.broadcasted_iota(jnp.int32, (r["hist"].shape[0], c2.shape[1]), 0)
+    times = jnp.zeros(node.shape, F32)
+    for k in range(r["n2"].shape[0]):
+        live = jnp.where(k < c2, r["n2"][k : k + 1, :], -1)
+        times = times + jnp.where(node == live, 1.0, 0.0)
+    total = dot_rows(r["hist"][...], times.astype(BF16))
+    agg2[...] = (total / c2.astype(F32)).astype(BF16)
+
+    store_own(own_n, dot(agg2[...], og[...]))
+    neigh.stage(0)
     r["back"][...] = lax.dot_general(
-        og[...], r["w2s"][...], (((1,), (1,)), ((), ())), preferred_element_type=F32
+        r["w2s"][...], og[...], (((1,), (1,)), ((), ())), preferred_element_type=F32
     )
-    later = dot(agg2[...], r["w2n"][...])
+    later = dot_rows(agg2[...], r["w2n"][...])
 
     pg, hid = r["pg"], r["hid"]
 
@@ -299,12 +315,17 @@
             chain.start(0, h)
         hid[span, :] = (pre * sig).astype(BF16)
 
-    store_own(own_s, dot_rows(hid[...], og[...]))
+    store_own(own_s, dot(hid[...], og[...]))
     itself.stage(0)
-    r["logits"][...] = (dot(hid[...], r["w2s"][...]) + later).astype(BF16)
+    r["logits"][...] = (dot_rows(hid[...], r["w2s"][...]) + later).astype(BF16)
 
     def term(c, block):
-        return dot(x[c], jnp.concatenate([block[0], block[1]], axis=0))
+        whole = jnp.concatenate([block[0], block[1]], axis=0)
+        return lax.dot_general(x[c], whole, (((1,), (1,)), ((), ())), preferred_element_type=F32)
+
+    def sums_on(point):
+        for which, number in PLAN[nz].get(point, ()):
+            (neigh if which == "n" else itself).stage(number)
 
     grad = term(z, pg)
     order = [("n", 0)] if near else []
@@ -319,44 +340,38 @@
                 chain.start(s + 1, h)
         for chain, offset in pair:
             grad = grad + term(wrap(z + offset), chain.arrived.at[s])
-        for number in AFTER_NEIGH_PLAN[nz].get(j, ()):
-            neigh.stage(number)
-        for number in SELF_PLAN[nz].get(j, ()):
-            itself.stage(number)
+        sums_on(j)
 
     own_g, rq, gy, go = r["own_g"], r["g_rq"], r["g_y"], r["g_o"]
     rows_g = own_g.shape[1]
     for j in range(nq):
-        own_g[j] = grad[j * rows_g : (j + 1) * rows_g]
+        own_g[j] = grad[j * rows_g : (j + 1) * rows_g].astype(BF16)
     first = group_q.copies((r["g_s0"], r["g_r0"]), lambda p: own_g.at[p], lambda o: rq.at[o - 1])
     for copy in first:
         copy.start()
-    for number in SELF_PLAN[nz].get("a", ()):
-        itself.stage(number)
-    total = own_g[q]
+    sums_on("a")
+    total = own_g[q].astype(F32)
     for o in range(nq - 1):
         first[o].wait_recv()
-        total = total + rq[o]
-    gy[y] = total
+        total = total + rq[o].astype(F32)
+    gy[y] = total.astype(BF16)
     second = group_y.copies((r["g_s1"], r["g_r1"]), lambda p: gy.at[y], lambda o: gy.at[y])
     for copy in second:
         copy.start()
-    for number in SELF_PLAN[nz].get("b", ()):
-        itself.stage(number)
+    sums_on("b")
     for chain in (red_rf, red_lf, red_rn, red_ln, all_rf, all_lf, all_rn, all_ln):
         chain.finish()
     neigh.stage(5)
     for copy in second:
         copy.wait_recv()
-    total = gy[0]
+    total = gy[0].astype(F32)
     for j in range(1, ny):
-        total = total + gy[j]
+        total = total + gy[j].astype(F32)
     go[q] = total
     third = group_q.copies((r["g_s2"], r["g_r2"]), lambda p: go.at[q], lambda o: go.at[q])
     for copy in third:
         copy.start()
-    for number in SELF_PLAN[nz].get("c", ()):
-        itself.stage(number)
+    sums_on("c")
     itself.stage(5)
     for copy in third:
         copy.wait_recv()
@@ -370,18 +385,21 @@
 TOTAL_NAMES = ("rxc", "vy", "ry", "vz", "fy", "fo") + tuple(
     f"{kind}{i}" for i in range(5) for kind in ("s", "r")
 )
-NEIGH_PLAN = {16: {0: (0,), 3: (1,), 6: (2,)}, 8: {0: (0,), 2: (1,)}}
-AFTER_NEIGH_PLAN = {16: {2: (3,), 5: (4,)}, 8: {0: (2,), 1: (3,), 2: (4,)}}
-SELF_PLAN = {
-    16: {3: (1,), 6: (2,), "b": (3,), "c": (4,)},
-    8: {0: (1,), 1: (2,), "b": (3,), "c": (4,)},
+PLAN = {
+    16: {2: ("n1",), 3: ("s1",), 4: ("n2",), 5: ("s2",), "a": ("n3", "s3"), "b": ("n4", "s4")},
+    8: {0: ("n1", "s1"), 1: ("n2", "s2"), "a": ("n3", "s3"), "b": ("n4", "s4")},
 }
+PLAN = {
+    size: {point: tuple((stage[0], int(stage[1])) for stage in stages) for point, stages in plan.items()}
+    for size, plan in PLAN.items()
+}
+INPUTS = ("f", "idx", "cnt", "tx", "w1s", "w1n", "hist", "n2", "c2", "og", "w2s", "w2n")
 
 
 def step(shape, idx, cnt, f, tx, hist, n2, c2, w1s, w1n, og, w2s, w2n):
     nz, ny, nq = shape
     targets, width = og.shape
-    half = targets // 2
+    half = width // 2
     deep = 2 * tx.shape[0]
     rows_q, rows_y, rows_g = width // nq, width // nq // ny, deep // nq
     jump = nz // 4
@@ -389,19 +407,19 @@
     V, D = pltpu.VMEM, pltpu.SemaphoreType.DMA
     scratch = dict(
         tab=V((f.shape[1] + 8, 128), F32),
-        rows=V((128, 128), F32),
+        rows=V((2, 128, 128), F32),
         x=V((nz, deep, 128), BF16),
-        w=V((deep, width), BF16),
-        agg2=V((targets, width), BF16),
-        part=V((nz, targets, width), F32),
-        pg=V((2, half, width), BF16),
-        hid=V((targets, width), BF16),
-        back=V((targets, width), F32),
+        w=V((width, deep), BF16),
+        agg2=V((width, targets), BF16),
+        part=V((nz, width, targets), F32),
+        pg=V((2, half, targets), BF16),
+        hid=V((width, targets), BF16),
+        back=V((width, targets), F32),
         own_n=V((nq, rows_q, width), F32),
         own_s=V((nq, rows_q, width), F32),
-        own_g=V((nq, rows_g, width), F32),
-        g_rq=V((nq - 1, rows_g, width), F32),
-        g_y=V((ny, rows_g, width), F32),
+        own_g=V((nq, rows_g, width), BF16),
+        g_rq=V((nq - 1, rows_g, width), BF16),
+        g_y=V((ny, rows_g, width), BF16),
         g_o=V((nq, rows_g, width), F32),
     )
     for i, size in enumerate((nq - 1, ny - 1, nq - 1)):
@@ -409,7 +427,7 @@
         scratch[f"g_r{i}"] = D((size,))
     for name, steps in lengths.items():
         for lead in ("out_", "in_", "ag_"):
-            scratch[lead + name] = V((steps, 2, half, width), BF16)
+            scratch[lead + name] = V((steps, 2, half, targets), BF16)
         for lead in ("rs_s", "rs_r", "ag_s", "ag_r"):
             scratch[lead + name] = D((steps, 2))
     for lead in ("n_", "s_"):
@@ -422,8 +440,12 @@
         for i, size in enumerate((nq, ny, nz, ny, nq)):
             scratch[lead + f"s{i}"] = D((size - 1,))
             scratch[lead + f"r{i}"] = D((size - 1,))
-    inputs = ("idx", "cnt", "f", "tx", "hist", "n2", "c2", "w1s", "w1n", "og", "w2s", "w2n")
-    names = inputs + ("logits", "g1", "gs", "gn") + tuple(scratch)
+    given = dict(f=f, idx=idx, cnt=cnt, tx=tx, w1s=w1s, w1n=w1n, hist=hist, n2=n2, c2=c2, og=og, w2s=w2s, w2n=w2n)
+    for name in INPUTS:
+        place = pltpu.SMEM if name == "idx" else V
+        scratch["v_" + name] = place(given[name].shape, given[name].dtype)
+    scratch["in_sem"] = D((len(INPUTS),))
+    names = INPUTS + ("logits", "g1", "gs", "gn") + tuple(scratch)
     vmem = pl.BlockSpec(memory_space=pltpu.VMEM)
     return pl.pallas_call(
         functools.partial(step_kernel, shape, names),
@@ -433,13 +455,13 @@
             jax.ShapeDtypeStruct((width, width), F32),
             jax.ShapeDtypeStruct((width, width), F32),
         ),
-        in_specs=[pl.BlockSpec(memory_space=pltpu.SMEM)] + [vmem] * (len(inputs) - 1),
+        in_specs=[pl.BlockSpec(memory_space=pl.ANY)] * len(INPUTS),
         out_specs=(vmem,) * 4,
         scratch_shapes=list(scratch.values()),
         compiler_params=pltpu.CompilerParams(
-            collective_id=0, has_side_effects=True, vmem_limit_bytes=40 << 20
+            collective_id=0, has_side_effects=True, vmem_limit_bytes=56 << 20
         ),
-    )(idx, cnt, f, tx, hist, n2, c2, w1s, w1n, og, w2s, w2n)
+    )(*[given[name] for name in INPUTS])
 
 
 def hand_out_kernel(logits, g1, gs, gn, o0, o1, o2, o3, o4):

time: 107 us -> 102 us (0.953)
  Pallas kernels: 99.6 us -> 95.4 us
  local copies, waits for them, and re-layouts: 5.37 us -> 4.29 us
    pallas_call x1, Pallas kernels: 98.7 us -> 94.5 us  [step(): pl.pallas_call(functools.partial(step_kernel, shape, names), out_shape=(j...]
    unnamed x22 -> x8, local copies, waits for them, and re-layouts: 5.35 us -> 3.64 us
where the time goes in v3:
time: 102 us; the launch traced here: 101 us
  Pallas kernels  95.4 us (94%)
  local copies, waits for them, and re-layouts  4.29 us (4%)
    pallas_call x1, Pallas kernels, step(): pl.pallas_call(functools.partial(step_kernel, shape, names), out_shape=(j...  94.5 us
    unnamed x8, local copies, waits for them, and re-layouts  3.64 us

profile of v3, /device:TPU:1, one launch (start us, length us, event | category | flops | bytes accessed | tf_op | source)
XLA Modules:
  0.0 101.3 jit_solution(2817699851037470443)
XLA Ops:
  0.6 0.9 fusion
  1.6 0.7 reshape.18.refs_1_
  2.2 94.5 %shard_map.155 = (bf16[128,256]{1,0:T(8,128)(2,1)}, f32[128,256]{1,0:T(8,128)}, f32[256,256]{1,0:T(8,128)}, f32[256,256]{1,0:T(8,128)}) custom-call(bf16[64,6144]{1,0:T(8,128)(2,1)} %refs_0_.1, s32[20480]{0:T(1024)} %reshape.18.refs_1_, s32[1,2048]{1,0:T(1,128)} %bitcast.2, bf16[64,2048]{1,0:T(8,128)(2,1)} %refs_3_.1, bf16[64,256]{1,0:T(8,128)(2,1)} %refs_4_.1, ...), custom_call_target="tpu_custom_call" | custom-call | tf_op jit(solution)/shard_map/pallas_call | solution.py:450
  96.7 0.0 copy-start
  96.7 0.9 copy-done
  97.7 0.0 copy-start.1
  97.7 0.9 copy-done.1
  98.6 0.0 copy-start.2
  98.6 0.9 copy-done.2
  99.5 0.0 copy-start.3
  99.5 0.8 copy-done.3
  100.4 0.9 shard_map.156
Async XLA Ops:
  96.7 1.0 copy-start
  97.7 0.9 copy-start.1
  98.6 0.9 copy-start.2
  99.5 0.8 copy-start.3

commit v4 on v3

--- a/solution.py
+++ b/solution.py
@@ -135,7 +135,7 @@
                 self.copy(s, h).wait_send()
 
 
-UNROLL = 16
+UNROLL = 32
 
 
 def step_kernel(shape, names, *refs):
@@ -464,25 +464,27 @@
     )(*[given[name] for name in INPUTS])
 
 
-def hand_out_kernel(logits, g1, gs, gn, o0, o1, o2, o3, o4):
+def hand_out_kernel(logits, g1, gs, gn, o0, o1, o2, o3, o4, sems):
     width = o1.shape[0]
-    o0[...] = logits[...]
-    o1[...] = g1[0:width, :]
-    o2[...] = g1[width:, :]
-    o3[...] = gs[...]
-    o4[...] = gn[...]
+    pairs = ((logits, o0), (g1.at[0:width], o1), (g1.at[width : 2 * width], o2), (gs, o3), (gn, o4))
+    copies = [pltpu.make_async_copy(a, b, sems.at[i]) for i, (a, b) in enumerate(pairs)]
+    for copy in copies:
+        copy.start()
+    for copy in copies:
+        copy.wait()
 
 
 def hand_out(logits, g1, gs, gn):
-    vmem = pl.BlockSpec(memory_space=pltpu.VMEM)
+    anywhere = pl.BlockSpec(memory_space=pl.ANY)
     like = lambda a: jax.ShapeDtypeStruct(a.shape, a.dtype)
     piece = jax.ShapeDtypeStruct((g1.shape[0] // 2, g1.shape[1]), F32)
     return pl.pallas_call(
         hand_out_kernel,
         out_shape=(like(logits), piece, piece, like(gs), like(gn)),
-        in_specs=[vmem] * 4,
-        out_specs=(vmem,) * 5,
-        compiler_params=pltpu.CompilerParams(vmem_limit_bytes=8 << 20),
+        in_specs=[anywhere] * 4,
+        out_specs=(anywhere,) * 5,
+        scratch_shapes=[pltpu.SemaphoreType.DMA((5,))],
+        compiler_params=pltpu.CompilerParams(vmem_limit_bytes=56 << 20),
     )(logits, g1, gs, gn)
 
 

time: 102 us -> 119 us (1.17)
  Pallas kernels: 95.4 us -> 117 us
  local copies, waits for them, and re-layouts: 4.29 us -> 0.65 us
    pallas_call x1, Pallas kernels: 0.9 us -> 23 us  [hand_out(): pl.pallas_call(hand_out_kernel, out_shape=(like(logits), piece, piece, li...]
    unnamed x8 -> x0, local copies, waits for them, and re-layouts: 3.64 us -> none
where the time goes in v4:
time: 119 us
  Pallas kernels  117 us (98%)
    pallas_call x1, Pallas kernels, step(): pl.pallas_call(functools.partial(step_kernel, shape, names), out_shape=(j...  94.1 us
    pallas_call x1, Pallas kernels, hand_out(): pl.pallas_call(hand_out_kernel, out_shape=(like(logits), piece, piece, li...  23 us

profile of v4, /device:TPU:1, one launch (start us, length us, event | category | flops | bytes accessed | tf_op | source)
XLA Modules:
  0.0 119.3 jit_solution(7281039114521622352)
XLA Ops:
  0.6 0.9 fusion
  1.6 0.7 reshape.18.refs_1_
  2.2 94.1 %shard_map.155 = (bf16[128,256]{1,0:T(8,128)(2,1)}, f32[128,256]{1,0:T(8,128)}, f32[256,256]{1,0:T(8,128)}, f32[256,256]{1,0:T(8,128)}) custom-call(bf16[64,6144]{1,0:T(8,128)(2,1)} %refs_0_.1, s32[20480]{0:T(1024)} %reshape.18.refs_1_, s32[1,2048]{1,0:T(1,128)} %bitcast.2, bf16[64,2048]{1,0:T(8,128)(2,1)} %refs_3_.1, bf16[64,256]{1,0:T(8,128)(2,1)} %refs_4_.1, ...), custom_call_target="tpu_custom_call" | custom-call | tf_op jit(solution)/shard_map/pallas_call | solution.py:450
  96.3 23.0 %shard_map.156 = (bf16[128,256]{1,0:T(8,128)(2,1)}, f32[64,256]{1,0:T(8,128)}, f32[64,256]{1,0:T(8,128)}, f32[256,256]{1,0:T(8,128)}, f32[256,256]{1,0:T(8,128)}) custom-call(bf16[128,256]{1,0:T(8,128)(2,1)} %get-tuple-element.9.logits, f32[128,256]{1,0:T(8,128)} %get-tuple-element.10.g1, f32[256,256]{1,0:T(8,128)} %get-tuple-element.11.gs, ...), custom_call_target="tpu_custom_call" | custom-call | tf_op jit(solution)/shard_map/pallas_call | solution.py:481
